TPU v7x, 32 devices: a whole 2x2x4 slice. The times are simulated.
32 devices in a mesh: rep: 2 (over y), tp: 16 (over z, x, core).
Axes of the slice: x: 2, y: 2, z: 4, core: 2. Of those that a mesh axis runs over, the one named last changes fastest.
Arguments:
- hidden: bfloat16 [64, 28672], P('rep', 'tp'), parts along dimension 0, may hold values from -6 to 6
- down_weight: bfloat16 [28672, 8192], P('tp'), may hold values from -0.03125 to 0.03125
- shrink_factor: bfloat16 [16, 64, 28672], P('tp'), may hold values from -0.03125 to 0.03125
- expand_factor: bfloat16 [16, 64, 8192], P('tp'), may hold values from -0.75 to 0.75
- variant_ids: int32 [64, 1], P('rep'), parts along dimension 0, may hold values from 0 to 15; in each aligned block of 32 rows (0 to 31, 32 to 63, ...) at most 8 rows name the same one
- owner: int32 [16], replicated, may hold values from 0 to 15, each once
Outputs:
- mixed: bfloat16 [64, 8192], P(('rep', 'tp')), parts along dimension 0
There are 2 independent parts, one for each index of `rep`. A program takes and returns all parts, laid end to end along the dimension named above; an argument that names none is the same for every part. Nothing has to cross between parts.
Inputs may be any that keep to these rules, and one draw needn't show every extreme that they name: `variant_ids`: every variant is named by at least one request and by at most 8; some variant by exactly 8. `owner`: each slot holds exactly one variant.
All inputs are finite; a program needn't handle non-finite values.
Results may differ from a plain program's by a relative error of at most 0.005.
Values may be sent and summed in bfloat16 or wider, within the bound.
A program may use at most 128 MiB of HBM per device.

v0:
```python
import jax
import jax.numpy as jnp
from jax import lax
from jax.sharding import PartitionSpec as P

CAP = 8


def local(hidden, down_weight, shrink_factor, expand_factor, variant_ids, owner):
    group_size = lax.axis_size("tp")
    my_index = lax.axis_index("tp")
    row_count = hidden.shape[0]
    col_count = hidden.shape[1]
    width_out = expand_factor.shape[2]
    rank_width = shrink_factor.shape[1]
    capacity = CAP
    variant_of = variant_ids[:, 0]
    holder = owner[variant_of]
    held_here = holder == my_index
    onehot = (variant_of[:, None] == jnp.arange(owner.shape[0], dtype=jnp.int32)[None, :]).astype(
        jnp.int32
    )
    earlier = jnp.cumsum(onehot, axis=0) - onehot
    order_in = jnp.sum(earlier * onehot, axis=1)
    request_index = jnp.arange(row_count, dtype=jnp.int32)
    slices = lax.all_to_all(shrink_factor, "tp", split_axis=2, concat_axis=0, tiled=True)
    all_rows = slices.reshape(group_size * rank_width, col_count)
    every_slot = lax.dot_general(
        hidden, all_rows, (((1,), (1,)), ((), ())), preferred_element_type=jnp.float32
    )
    every_slot = every_slot.reshape(row_count, group_size, rank_width)
    chosen = holder[:, None] == jnp.arange(group_size, dtype=jnp.int32)[None, :]
    partial_value = jnp.sum(jnp.where(chosen[:, :, None], every_slot, jnp.float32(0.0)), axis=1)
    shrunk = lax.psum(partial_value, "tp").astype(jnp.bfloat16)
    source = jnp.full((capacity,), row_count, jnp.int32)
    source = source.at[jnp.where(held_here, order_in, capacity)].set(request_index, mode="drop")
    padded_shrunk = jnp.concatenate([shrunk, jnp.zeros((1, shrunk.shape[1]), jnp.bfloat16)], axis=0)
    delta_rows = jnp.dot(
        padded_shrunk[source], expand_factor[0], preferred_element_type=jnp.float32
    ).astype(jnp.bfloat16)
    delta_table = jnp.concatenate([delta_rows, jnp.zeros((1, width_out), jnp.bfloat16)], axis=0)
    pick_index = jnp.where(held_here, order_in, capacity)
    block_base = jnp.dot(hidden, down_weight, preferred_element_type=jnp.float32)
    summed = lax.psum_scatter(
        block_base + delta_table[pick_index].astype(jnp.float32),
        "tp",
        scatter_dimension=0,
        tiled=True,
    )
    return summed.astype(jnp.bfloat16)


def solution(mesh):
    in_specs = (
        P("rep", "tp"),
        P("tp", None),
        P("tp", None, None),
        P("tp", None, None),
        P("rep", None),
        P(),
    )
    out_specs = P(("rep", "tp"), None)
    return jax.shard_map(local, mesh=mesh, in_specs=in_specs, out_specs=out_specs, check_vma=False)
```

profile of v0, /device:TPU:0, one launch (start us, length us, event | category | flops | bytes accessed | tf_op | source)
XLA Modules:
  0.0 468.9 jit_solution(4445458359268457077)
XLA Ops:
  0.0 0.0 copy-start
  0.0 29.0 %copy.8 = bf16[1,64,28672]{1,0,2:T(2,128)(2,1)} copy(bf16[1,64,28672]{2,1,0:T(8,128)(2,1)} %param.8) | data formatting | bytes 7340032 | tf_op args[2]
  29.1 0.5 broadcast.111
  29.6 157.1 %reduce = bf16[28672,64]{1,0:T(8,128)(2,1)} reduce(bf16[28672,1,64]{2,1,0:T(2,128)(2,1)} %bitcast.32, bf16[]{:T(256)} %broadcast.111), dimensions={1}, to_apply=%bitcast.26.reduce_sub_computation | reduce | bytes 7340034
  186.6 0.0 copy-start.3
  186.6 0.0 copy-start.1
  186.6 0.0 copy-start.4
  186.6 13.4 %reshape.105 = bf16[16,2,57344]{2,1,0:T(2,128)(2,1)} reshape(bf16[28672,64]{1,0:T(8,128)(2,1)} %reduce) | data formatting | bytes 7340032
  200.0 7.4 %all-to-all-start = ((bf16[16,2,57344]{2,1,0:T(2,128)(2,1)}), bf16[16,2,57344]{2,1,0:T(2,128)(2,1)}, u32[]{:S(2)}, u32[]{:S(2)}) async-start(bf16[16,2,57344]{2,1,0:T(2,128)(2,1)} %reshape.105), calls=%async_computation | async-start | bytes 7340032 | tf_op jit(solution)/shard_map/all_to_all | solution.py:26
  207.4 0.0 copy-done.3
  207.4 0.0 copy-done.1
  207.5 0.7 gather_fusion
  208.2 0.1 fusion.10
  208.2 0.1 reduce_window_sum.11
  208.3 0.0 copy-done.4
  208.3 0.6 dynamic-slice
  209.5 0.2 select_reduce_fusion
  209.7 0.7 scatter_custom_fusion
  210.5 65.5 %all-to-all-done = bf16[16,2,57344]{2,1,0:T(2,128)(2,1)} async-done(((bf16[16,2,57344]{2,1,0:T(2,128)(2,1)}), bf16[16,2,57344]{2,1,0:T(2,128)(2,1)}, u32[]{:S(2)}, u32[]{:S(2)}) %all-to-all-start) | async-done | bytes 3670048 | tf_op jit(solution)/shard_map/all_to_all | solution.py:26
  276.0 14.2 %reshape.106 = bf16[28672,1,64]{2,1,0:T(2,128)(2,1)} reshape(bf16[16,2,57344]{2,1,0:T(2,128)(2,1)} %all-to-all-done) | data formatting | bytes 7340032
  290.1 9.6 %copy.13 = bf16[1,64,28672]{1,2,0:T(8,128)(2,1)} copy(bf16[1,64,28672]{1,0,2:T(2,128)(2,1)} %bitcast.33) | data formatting | bytes 7340032
  299.8 0.0 copy-start.2
  299.8 8.0 %copy.10 = bf16[1,64,16,1792]{3,1,2,0:T(8,128)(2,1)} copy(bf16[1,64,16,1792]{1,3,2,0:T(8,128)(2,1)} %bitcast.34) | data formatting | bytes 7340032 | tf_op jit(solution)/shard_map/all_to_all | solution.py:26
  307.8 0.0 copy-done.2
  307.8 3.8 fusion.5
  311.6 73.6 %psum.7 = bf16[32,64]{1,0:T(8,128)(2,1)S(1)} all-reduce(f32[32,64]{1,0:T(8,128)S(1)} %fusion.5), channel_id=1, replica_groups=mesh['rep'=2,'tp'=16] {'tp'}, use_global_device_ids=true, to_apply=%region_1.2 | all-reduce | flops 2048 | bytes 12288 | tf_op jit(solution)/shard_map/psum | solution.py:34
  385.2 0.6 gather_fusion.1
  385.8 0.0 copy-done
  385.8 0.2 convolution_convert_fusion
  386.0 0.9 gather_fusion.2
  386.9 12.0 %convolution_add_fusion = f32[32,8192]{1,0:T(8,128)S(1)} fusion(bf16[32,1792]{1,0:T(8,128)(2,1)S(1)} %copy-done.2, bf16[1792,8192]{1,0:T(8,128)(2,1)} %param.7, bf16[32,8192]{1,0:T(8,128)(2,1)S(1)} %gather_fusion.2), kind=kOutput, calls=%fused_computation.4 | convolution fusion | flops 940048384 | bytes 31047680 | tf_op jit(solution)/shard_map/dot_general | solution.py:43
  398.9 69.3 %all-reduce.4 = bf16[32,8192]{1,0:T(8,128)(2,1)S(1)} all-reduce(f32[32,8192]{1,0:T(8,128)S(1)} %convolution_add_fusion), channel_id=2, replica_groups=mesh['rep'=2,'tp'=16] {'tp'}, use_global_device_ids=true, to_apply=%region_5.6.clone | all-reduce | flops 262144 | bytes 1572864
  468.3 0.7 dynamic-slice_convert_fusion
  (11 shorter events, 0.1 us)
Async XLA Ops:
  0.0 385.8 %copy-start = (bf16[1,64,8192]{2,1,0:T(8,128)(2,1)S(1)}, bf16[1,64,8192]{2,1,0:T(8,128)(2,1)}, u32[]{:S(2)}) copy-start(bf16[1,64,8192]{2,1,0:T(8,128)(2,1)} %param.9) | copy-start | bytes 3145732
  186.6 20.8 %copy-start.3 = (s32[32,1]{0,1:T(1,128)S(1)}, s32[32,1]{0,1:T(1,128)}, u32[]{:S(2)}) copy-start(s32[32,1]{0,1:T(1,128)} %param.10) | copy-start | bytes 388
  186.6 20.8 %copy-start.1 = (s32[16]{0:T(128)S(1)}, s32[16]{0:T(128)}, u32[]{:S(2)}) copy-start(s32[16]{0:T(128)} %param.11) | copy-start | bytes 196
  186.6 21.7 %copy-start.4 = (u32[32]{0:T(128)S(1)}, u32[32]{0:T(128)}, u32[]{:S(2)}) copy-start(u32[32]{0:T(128)} %constant.36) | copy-start | bytes 388
  200.0 76.0 %all-to-all-start = ((bf16[16,2,57344]{2,1,0:T(2,128)(2,1)}), bf16[16,2,57344]{2,1,0:T(2,128)(2,1)}, u32[]{:S(2)}, u32[]{:S(2)}) async-start(bf16[16,2,57344]{2,1,0:T(2,128)(2,1)} %reshape.105), calls=%async_computation | async-start | bytes 7340032 | tf_op jit(solution)/shard_map/all_to_all | solution.py:26
  299.8 8.0 %copy-start.2 = (bf16[32,1792]{1,0:T(8,128)(2,1)S(1)}, bf16[32,1792]{1,0:T(8,128)(2,1)}, u32[]{:S(2)}) copy-start(bf16[32,1792]{1,0:T(8,128)(2,1)} %param.6) | copy-start | bytes 344068
where the time goes:
time: 472 us; the launch traced here: 469 us
  other arithmetic  157 us (33%)
  blocking collectives  143 us (30%)
  local copies, waits for them, and re-layouts  78.9 us (17%)
  waiting for transfers between devices  65.5 us (14%)
  matrix products  16 us (3%)
  starting transfers between devices  7.4 us (2%)
    unnamed x1, other arithmetic  157 us
    psum x1, blocking collectives, local(): shrunk = lax.psum(partial_value, 'tp').astype(jnp.bfloat16)  73.6 us
    unnamed x1, blocking collectives  69.3 us
    unnamed x16, local copies, waits for them, and re-layouts  67.3 us
    all_to_all x1, waiting for transfers between devices, local(): lax.all_to_all(shrink_factor, 'tp', split_axis=2, concat_axis=0, tiled=True)  65.5 us
    dot_general x1, matrix products, local(): jnp.dot(hidden, down_weight, preferred_element_type=jnp.float32)  12 us
  transfers between devices with their start and end apart: 1, of which 1 were waited for; matrix products, arithmetic and copies ran while one was open for 0% of the time, Pallas kernels for 0%

commit v1 on v0

--- a/solution.py
+++ b/solution.py
@@ -1,12 +1,244 @@
+import functools
+
 import jax
 import jax.numpy as jnp
 from jax import lax
+from jax.experimental import pallas as pl
+from jax.experimental.pallas import tpu as pltpu
 from jax.sharding import PartitionSpec as P
 
 CAP = 8
-
-
-def local(hidden, down_weight, shrink_factor, expand_factor, variant_ids, owner):
+F32 = jnp.float32
+BF16 = jnp.bfloat16
+MESH = pl.DeviceIdType.MESH
+
+
+def iota(shape, axis):
+    return lax.broadcasted_iota(jnp.int32, shape, axis)
+
+
+def log2(n):
+    return n.bit_length() - 1
+
+
+def contract(a, b, da, db):
+    return lax.dot_general(a, b, (((da,), (db,)), ((), ())), preferred_element_type=F32)
+
+
+def kernel(n, chunks, vid, own, hid, w_hbm, s_hbm, e_hbm, out, wbuf, sbuf, ebuf, hperm, snd, rcv,
+           part, arcv, bsnd, brcv, keep, csnd, crcv, wsem, ssem, esem, dss, drs, asem, arem, bsem,
+           brem, csem, crem):
+    me = lax.axis_index("tp")
+    core, x, z = lax.rem(me, 2), lax.rem(me // 2, 2), me // 4
+    nz = n // 4
+    rows, cols = hid.shape
+    per = rows // n
+    group = nz * per
+    half = cols // 2
+    wide = wbuf.shape[2]
+    folds = 16 // per
+    narrow = wide // folds
+
+    def load_w(c):
+        at = pl.ds(pl.multiple_of(c * wide, wide), wide)
+        return pltpu.make_async_copy(w_hbm.at[:, at], wbuf.at[c], wsem.at[c])
+
+    load_s = pltpu.make_async_copy(s_hbm.at[0], sbuf, ssem)
+    load_e = pltpu.make_async_copy(e_hbm.at[0], ebuf, esem)
+    for c in range(chunks):
+        load_w(c).start()
+    load_s.start()
+    load_e.start()
+
+    barrier = pltpu.get_barrier_semaphore()
+
+    @pl.loop(1, n)
+    def _(d):
+        pl.semaphore_signal(barrier, inc=1, device_id={"tp": lax.rem(me + d, n)}, device_id_type=MESH)
+
+    variants = own.shape[1]
+    named = vid[...] == iota((rows, variants), 1)
+    holder = jnp.sum(jnp.where(named, own[...].astype(F32), 0.0), axis=1, keepdims=True)
+    named = named.astype(F32).astype(BF16)
+    same = contract(named, named, 1, 1)
+    earlier = iota((rows, rows), 1) < iota((rows, rows), 0)
+    order = jnp.sum(jnp.where(earlier, same, 0.0), axis=1, keepdims=True)
+    slot = holder * CAP + order
+    place = (slot == iota((rows, n * CAP), 1).astype(F32)).astype(F32).astype(BF16)
+    halves = [
+        contract(place, hid[:, h * half:(h + 1) * half], 0, 0).reshape(n, CAP, half) for h in range(2)
+    ]
+    snd[...] = jnp.concatenate(halves, axis=1).astype(BF16)
+    rcv[0] = snd[me]
+
+    at = iota((rows, rows), 0)
+    r = at & (per - 1)
+    z_of = lax.shift_right_logical(at, log2(per)) & (nz - 1)
+    x_of = lax.shift_right_logical(at, log2(group)) & 1
+    core_of = lax.shift_right_logical(at, log2(group) + 1)
+    reorder = (((z_of * 2 + x_of) * 2 + core_of) * per + r == iota((rows, rows), 1))
+    reorder = reorder.astype(F32).astype(BF16)
+    hperm[...] = contract(reorder, hid[...], 1, 0).astype(BF16)
+    mine = (slot == (iota((rows, CAP), 1) + me * CAP).astype(F32)).astype(F32).astype(BF16)
+    spread = contract(reorder, mine, 1, 0).astype(BF16)
+
+    pl.semaphore_wait(barrier, n - 1)
+
+    def dispatch(d):
+        to = lax.rem(me + d, n)
+        return pltpu.make_async_remote_copy(
+            src_ref=snd.at[to], dst_ref=rcv.at[d], send_sem=dss.at[d], recv_sem=drs.at[d],
+            device_id={"tp": to}, device_id_type=MESH)
+
+    @pl.loop(1, n)
+    def _(d):
+        dispatch(d).start()
+
+    @pl.loop(0, chunks)
+    def _(c):
+        load_w(c).wait()
+        total = jnp.dot(hperm[...], wbuf[c], preferred_element_type=F32)
+        part[c] = total.reshape(2, 2, group, wide)
+
+    load_s.wait()
+
+    def shrink(d, total):
+        start = lax.rem(me - d + n, n) * cols
+        got = rcv[d]
+        first = sbuf[:, pl.ds(pl.multiple_of(start, half), half)]
+        second = sbuf[:, pl.ds(pl.multiple_of(start + half, half), half)]
+        return total + contract(got, first, 1, 1)[:CAP] + contract(got, second, 1, 1)[CAP:]
+
+    def arrived(d, total):
+        dispatch(d).wait_recv()
+        return shrink(d, total)
+
+    shrunk = shrink(0, jnp.zeros((CAP, sbuf.shape[0]), F32))
+    shrunk = lax.fori_loop(1, n, arrived, shrunk).astype(BF16)
+    shrunk = contract(spread, shrunk, 1, 0).astype(BF16)
+    load_e.wait()
+
+    def to_core(c):
+        return pltpu.make_async_remote_copy(
+            src_ref=part.at[c, 1 - core], dst_ref=arcv.at[c], send_sem=asem.at[c],
+            recv_sem=arem.at[c], device_id={"tp": me + 1 - 2 * core}, device_id_type=MESH)
+
+    def to_x(c):
+        return pltpu.make_async_remote_copy(
+            src_ref=bsnd.at[c], dst_ref=brcv.at[c], send_sem=bsem.at[c], recv_sem=brem.at[c],
+            device_id={"tp": me + 2 - 4 * x}, device_id_type=MESH)
+
+    def to_z(c, d):
+        to = lax.rem(z + d, nz)
+        return pltpu.make_async_remote_copy(
+            src_ref=csnd.at[c, to], dst_ref=crcv.at[c, d - 1], send_sem=csem.at[c, d - 1],
+            recv_sem=crem.at[c, d - 1], device_id={"tp": me + (to - z) * 4}, device_id_type=MESH)
+
+    @pl.loop(0, chunks)
+    def _(c):
+        at = pl.ds(pl.multiple_of(c * wide, wide), wide)
+        delta = jnp.dot(shrunk, ebuf[:, at], preferred_element_type=F32).astype(BF16).astype(F32)
+        part[c] = part[c] + delta.reshape(2, 2, group, wide)
+        to_core(c).start()
+
+    @pl.loop(0, chunks)
+    def _(c):
+        to_core(c).wait_recv()
+        away = part[c, core, 1 - x] + arcv[c, 1 - x]
+        away = jnp.concatenate([away[:, :wide // 2], away[:, wide // 2:]], axis=0)
+        bsnd[c] = away.astype(BF16)
+        to_x(c).start()
+        keep[c] = part[c, core, x] + arcv[c, x]
+
+    size = folds * group
+    at = iota((size, size), 0)
+    r = at & (per - 1)
+    fold = lax.shift_right_logical(at, log2(per)) & (folds - 1)
+    z_of = lax.shift_right_logical(at, log2(per * folds))
+    refold = ((fold * nz + z_of) * per + r == iota((size, size), 1)).astype(F32).astype(BF16)
+
+    @pl.loop(0, chunks)
+    def _(c):
+        to_x(c).wait_recv()
+        got = brcv[c].astype(F32)
+        total = keep[c] + jnp.concatenate([got[:group], got[group:]], axis=1)
+        folded = jnp.concatenate(
+            [total[:, j * narrow:(j + 1) * narrow] for j in range(folds)], axis=0).astype(BF16)
+        csnd[c] = contract(refold, folded, 1, 0).astype(BF16).reshape(nz, 16, narrow)
+        for d in range(1, nz):
+            to_z(c, d).start()
+
+    @pl.loop(0, chunks)
+    def _(c):
+        total = csnd[c, z].astype(F32)
+        for d in range(1, nz):
+            to_z(c, d).wait_recv()
+            total = total + crcv[c, d - 1].astype(F32)
+        row = jnp.concatenate([total[j * per:(j + 1) * per] for j in range(folds)], axis=1)
+        out[:, pl.ds(pl.multiple_of(c * wide, wide), wide)] = row.astype(BF16)
+
+    @pl.loop(1, n)
+    def _(d):
+        dispatch(d).wait_send()
+
+    @pl.loop(0, chunks)
+    def _(c):
+        to_core(c).wait_send()
+        to_x(c).wait_send()
+        for d in range(1, nz):
+            to_z(c, d).wait_send()
+
+
+def fits(n, rows, cols, width):
+    per = rows // n
+    return (n % 4 == 0 and cols % 256 == 0 and width % 1024 == 0 and per in (1, 2, 4, 8, 16)
+            and rows == n * per and (n // 4) * per == 8)
+
+
+def fused(hidden, down_weight, shrink_factor, expand_factor, variant_ids, owner):
+    n = lax.axis_size("tp")
+    rows, cols = hidden.shape
+    rank, depth = shrink_factor.shape[1:]
+    width = down_weight.shape[1]
+    wide = 1024
+    chunks = width // wide
+    nz = n // 4
+    per = rows // n
+    group = nz * per
+    narrow = wide * per // 16
+    vmem = pl.BlockSpec(memory_space=pltpu.VMEM)
+    hbm = pl.BlockSpec(memory_space=pl.ANY)
+    dma = pltpu.SemaphoreType.DMA
+    return pl.pallas_call(
+        functools.partial(kernel, n, chunks),
+        out_shape=jax.ShapeDtypeStruct((per, width), BF16),
+        in_specs=[vmem, vmem, vmem, hbm, hbm, hbm],
+        out_specs=vmem,
+        scratch_shapes=[
+            pltpu.VMEM((chunks, cols, wide), BF16),
+            pltpu.VMEM((rank, depth), BF16),
+            pltpu.VMEM((rank, width), BF16),
+            pltpu.VMEM((rows, cols), BF16),
+            pltpu.VMEM((n, 2 * CAP, cols // 2), BF16),
+            pltpu.VMEM((n, 2 * CAP, cols // 2), BF16),
+            pltpu.VMEM((chunks, 2, 2, group, wide), F32),
+            pltpu.VMEM((chunks, 2, group, wide), F32),
+            pltpu.VMEM((chunks, 2 * group, wide // 2), BF16),
+            pltpu.VMEM((chunks, 2 * group, wide // 2), BF16),
+            pltpu.VMEM((chunks, group, wide), F32),
+            pltpu.VMEM((chunks, nz, 16, narrow), BF16),
+            pltpu.VMEM((chunks, nz - 1, 16, narrow), BF16),
+            dma((chunks,)), dma(()), dma(()), dma((n,)), dma((n,)),
+            dma((chunks,)), dma((chunks,)), dma((chunks,)), dma((chunks,)),
+            dma((chunks, nz - 1)), dma((chunks, nz - 1)),
+        ],
+        compiler_params=pltpu.CompilerParams(
+            collective_id=0, has_side_effects=True, vmem_limit_bytes=56 * 2**20),
+        name="fused",
+    )(variant_ids, owner.reshape(1, -1), hidden, down_weight, shrink_factor, expand_factor)
+
+
+def general(hidden, down_weight, shrink_factor, expand_factor, variant_ids, owner):
     group_size = lax.axis_size("tp")
     my_index = lax.axis_index("tp")
     row_count = hidden.shape[0]
@@ -50,6 +282,12 @@
     return summed.astype(jnp.bfloat16)
 
 
+def local(hidden, down_weight, shrink_factor, expand_factor, variant_ids, owner):
+    n = lax.axis_size("tp")
+    form = fused if fits(n, *hidden.shape, down_weight.shape[1]) else general
+    return form(hidden, down_weight, shrink_factor, expand_factor, variant_ids, owner)
+
+
 def solution(mesh):
     in_specs = (
         P("rep", "tp"),

time: 472 us -> 34.7 us (0.07)
  other arithmetic: 157 us -> 0 us
  blocking collectives: 143 us -> 0 us
  local copies, waits for them, and re-layouts: 78.9 us -> 2.74 us
  waiting for transfers between devices: 65.5 us -> 0 us
  Pallas kernels: 0 us -> 31.8 us
  matrix products: 16 us -> 0 us
  starting transfers between devices: 7.4 us -> 0 us
    unnamed x1 -> x0, other arithmetic: 157 us -> none
    psum x1 -> x0, blocking collectives: 73.6 us -> none  [local(): shrunk = lax.psum(partial_value, 'tp').astype(jnp.bfloat16)]
    unnamed x1 -> x0, blocking collectives: 69.3 us -> none
    all_to_all x1 -> x0, waiting for transfers between devices: 65.5 us -> none  [local(): lax.all_to_all(shrink_factor, 'tp', split_axis=2, concat_axis=0, tiled=True)]
    unnamed x16 -> x2, local copies, waits for them, and re-layouts: 67.3 us -> 2.74 us
    pallas_call x0 -> x1, Pallas kernels: none -> 31.8 us  [fused(): pl.pallas_call(functools.partial(kernel, n, chunks), out_shape=jax.ShapeD...]
    dot_general x3 -> x0, matrix products: 16 us -> none  [the longest x1 12 us: local(): jnp.dot(hidden, down_weight, preferred_element_type=jnp.float32)]
    all_to_all x1 -> x0, local copies, waits for them, and re-layouts: 8.02 us -> none  [local(): lax.all_to_all(shrink_factor, 'tp', split_axis=2, concat_axis=0, tiled=True)]
  transfers between devices with their start and end apart: 1 -> 0, of which waited for: 1 -> 0; matrix products, arithmetic and copies ran while one was open for 0% -> 0% of each run, Pallas kernels for 0% -> 0%
where the time goes in v1:
time: 34.7 us; the launch traced here: 34.5 us
  Pallas kernels  31.8 us (92%)
  local copies, waits for them, and re-layouts  2.74 us (8%)
    pallas_call x1, Pallas kernels, fused(): pl.pallas_call(functools.partial(kernel, n, chunks), out_shape=jax.ShapeD...  31.8 us
    unnamed x2, local copies, waits for them, and re-layouts  2.74 us

profile of v1, /device:TPU:0, one launch (start us, length us, event | category | flops | bytes accessed | tf_op | source)
XLA Modules:
  0.0 34.5 jit_solution(842922966076175866)
XLA Ops:
  0.0 1.3 %copy.7.vid = s32[32,1]{1,0:T(8,128)} copy(s32[32,1]{0,1:T(1,128)} %param.10) | data formatting | bytes 256 | tf_op args[4]
  1.3 31.8 %fused.1 = bf16[2,8192]{1,0:T(2,128)(2,1)} custom-call(s32[32,1]{1,0:T(8,128)} %copy.7.vid, s32[1,16]{1,0:T(1,128)} %bitcast.1, bf16[32,1792]{1,0:T(8,128)(2,1)} %hid.1, bf16[1792,8192]{1,0:T(8,128)(2,1)} %w_hbm.1, bf16[1,64,28672]{2,1,0:T(8,128)(2,1)} %s_hbm.1, bf16[1,64,8192]{2,1,0:T(8,128)(2,1)} %e_hbm.1), custom_call_target="tpu_custom_call" | custom-call | tf_op jit(solution)/shard_map/fused/pallas_call | solution.py:212
  33.1 1.4 %copy.9 = bf16[2,8192]{1,0:T(2,128)(2,1)} copy(bf16[2,8192]{1,0:T(2,128)(2,1)} %fused.1) | data formatting | bytes 65536

commit v2 on v1

--- a/solution.py
+++ b/solution.py
@@ -57,16 +57,16 @@
         pl.semaphore_signal(barrier, inc=1, device_id={"tp": lax.rem(me + d, n)}, device_id_type=MESH)
 
     variants = own.shape[1]
-    named = vid[...] == iota((rows, variants), 1)
-    holder = jnp.sum(jnp.where(named, own[...].astype(F32), 0.0), axis=1, keepdims=True)
+    named = vid[...] == iota((variants, rows), 0)
     named = named.astype(F32).astype(BF16)
-    same = contract(named, named, 1, 1)
-    earlier = iota((rows, rows), 1) < iota((rows, rows), 0)
-    order = jnp.sum(jnp.where(earlier, same, 0.0), axis=1, keepdims=True)
+    holder = contract(own[...].astype(F32).astype(BF16), named, 1, 0)
+    same = contract(named, named, 0, 0)
+    earlier = iota((rows, rows), 0) < iota((rows, rows), 1)
+    order = jnp.sum(jnp.where(earlier, same, 0.0), axis=0, keepdims=True)
     slot = holder * CAP + order
-    place = (slot == iota((rows, n * CAP), 1).astype(F32)).astype(F32).astype(BF16)
+    place = (slot == iota((n * CAP, rows), 0).astype(F32)).astype(F32).astype(BF16)
     halves = [
-        contract(place, hid[:, h * half:(h + 1) * half], 0, 0).reshape(n, CAP, half) for h in range(2)
+        contract(place, hid[:, h * half:(h + 1) * half], 1, 0).reshape(n, CAP, half) for h in range(2)
     ]
     snd[...] = jnp.concatenate(halves, axis=1).astype(BF16)
     rcv[0] = snd[me]
@@ -79,8 +79,8 @@
     reorder = (((z_of * 2 + x_of) * 2 + core_of) * per + r == iota((rows, rows), 1))
     reorder = reorder.astype(F32).astype(BF16)
     hperm[...] = contract(reorder, hid[...], 1, 0).astype(BF16)
-    mine = (slot == (iota((rows, CAP), 1) + me * CAP).astype(F32)).astype(F32).astype(BF16)
-    spread = contract(reorder, mine, 1, 0).astype(BF16)
+    mine = (slot == (iota((CAP, rows), 0) + me * CAP).astype(F32)).astype(F32).astype(BF16)
+    spread = contract(reorder, mine, 1, 1).astype(BF16)
 
     pl.semaphore_wait(barrier, n - 1)
 
@@ -90,9 +90,11 @@
             src_ref=snd.at[to], dst_ref=rcv.at[d], send_sem=dss.at[d], recv_sem=drs.at[d],
             device_id={"tp": to}, device_id_type=MESH)
 
-    @pl.loop(1, n)
-    def _(d):
-        dispatch(d).start()
+    order_out = ((n // 2, n), (n // 4, n // 2), (1, n // 4))
+    for first, last in order_out:
+        @pl.loop(first, last)
+        def _(d):
+            dispatch(d).start()
 
     @pl.loop(0, chunks)
     def _(c):
@@ -114,8 +116,9 @@
         return shrink(d, total)
 
     shrunk = shrink(0, jnp.zeros((CAP, sbuf.shape[0]), F32))
-    shrunk = lax.fori_loop(1, n, arrived, shrunk).astype(BF16)
-    shrunk = contract(spread, shrunk, 1, 0).astype(BF16)
+    for first, last in order_out:
+        shrunk = lax.fori_loop(first, last, arrived, shrunk)
+    shrunk = contract(spread, shrunk.astype(BF16), 1, 0).astype(BF16)
     load_e.wait()
 
     def to_core(c):
@@ -191,7 +194,7 @@
 
 def fits(n, rows, cols, width):
     per = rows // n
-    return (n % 4 == 0 and cols % 256 == 0 and width % 1024 == 0 and per in (1, 2, 4, 8, 16)
+    return (n % 4 == 0 and n <= 256 and cols % 256 == 0 and width % 2048 == 0 and per in (1, 2, 4, 8, 16)
             and rows == n * per and (n // 4) * per == 8)
 
 
@@ -200,7 +203,7 @@
     rows, cols = hidden.shape
     rank, depth = shrink_factor.shape[1:]
     width = down_weight.shape[1]
-    wide = 1024
+    wide = 2048
     chunks = width // wide
     nz = n // 4
     per = rows // n
@@ -235,7 +238,7 @@
         compiler_params=pltpu.CompilerParams(
             collective_id=0, has_side_effects=True, vmem_limit_bytes=56 * 2**20),
         name="fused",
-    )(variant_ids, owner.reshape(1, -1), hidden, down_weight, shrink_factor, expand_factor)
+    )(variant_ids.reshape(1, -1), owner.reshape(1, -1), hidden, down_weight, shrink_factor, expand_factor)
 
 
 def general(hidden, down_weight, shrink_factor, expand_factor, variant_ids, owner):

time: 34.7 us -> 32.1 us (0.925)
  local copies, waits for them, and re-layouts: 2.74 us -> 1.4 us
  Pallas kernels: 31.8 us -> 30.5 us
    unnamed x2 -> x1, local copies, waits for them, and re-layouts: 2.74 us -> 1.4 us
    pallas_call x1, Pallas kernels: 31.8 us -> 30.5 us  [fused(): pl.pallas_call(functools.partial(kernel, n, chunks), out_shape=jax.ShapeD...]
where the time goes in v2:
time: 32.1 us; the launch traced here: 31.9 us
  Pallas kernels  30.5 us (95%)
  local copies, waits for them, and re-layouts  1.4 us (4%)
    pallas_call x1, Pallas kernels, fused(): pl.pallas_call(functools.partial(kernel, n, chunks), out_shape=jax.ShapeD...  30.5 us
    unnamed x1, local copies, waits for them, and re-layouts  1.4 us

profile of v2, /device:TPU:0, one launch (start us, length us, event | category | flops | bytes accessed | tf_op | source)
XLA Modules:
  0.0 31.9 jit_solution(9943558194949680828)
XLA Ops:
  0.0 30.5 %fused.1 = bf16[2,8192]{1,0:T(2,128)(2,1)} custom-call(s32[1,32]{1,0:T(1,128)} %bitcast.2, s32[1,16]{1,0:T(1,128)} %bitcast.3, bf16[32,1792]{1,0:T(8,128)(2,1)} %hid.1, bf16[1792,8192]{1,0:T(8,128)(2,1)} %w_hbm.1, bf16[1,64,28672]{2,1,0:T(8,128)(2,1)} %s_hbm.1, bf16[1,64,8192]{2,1,0:T(8,128)(2,1)} %e_hbm.1), custom_call_target="tpu_custom_call" | custom-call | tf_op jit(solution)/shard_map/fused/pallas_call | solution.py:215
  30.5 1.4 %copy.8 = bf16[2,8192]{1,0:T(2,128)(2,1)} copy(bf16[2,8192]{1,0:T(2,128)(2,1)} %fused.1) | data formatting | bytes 65536

commit v3 on v2

--- a/solution.py
+++ b/solution.py
@@ -90,7 +90,7 @@
             src_ref=snd.at[to], dst_ref=rcv.at[d], send_sem=dss.at[d], recv_sem=drs.at[d],
             device_id={"tp": to}, device_id_type=MESH)
 
-    order_out = ((n // 2, n), (n // 4, n // 2), (1, n // 4))
+    order_out = ((1, n // 4), (n // 2, n), (n // 4, n // 2))
     for first, last in order_out:
         @pl.loop(first, last)
         def _(d):
@@ -104,21 +104,25 @@
 
     load_s.wait()
 
-    def shrink(d, total):
+    def shrink(d, totals):
         start = lax.rem(me - d + n, n) * cols
         got = rcv[d]
         first = sbuf[:, pl.ds(pl.multiple_of(start, half), half)]
         second = sbuf[:, pl.ds(pl.multiple_of(start + half, half), half)]
-        return total + contract(got, first, 1, 1)[:CAP] + contract(got, second, 1, 1)[CAP:]
-
-    def arrived(d, total):
-        dispatch(d).wait_recv()
-        return shrink(d, total)
-
-    shrunk = shrink(0, jnp.zeros((CAP, sbuf.shape[0]), F32))
+        return totals[0] + contract(got, first, 1, 1), totals[1] + contract(got, second, 1, 1)
+
+    zero = jnp.zeros((2 * CAP, sbuf.shape[0]), F32)
+    totals = shrink(0, (zero, zero))
     for first, last in order_out:
-        shrunk = lax.fori_loop(first, last, arrived, shrunk)
-    shrunk = contract(spread, shrunk.astype(BF16), 1, 0).astype(BF16)
+        @pl.loop(first, last)
+        def _(d):
+            dispatch(d).wait_recv()
+
+        for d in range(first, last):
+            totals = shrink(d, totals)
+    top, low = totals
+    shrunk = (top[:CAP] + low[CAP:]).astype(BF16)
+    shrunk = contract(spread, shrunk, 1, 0).astype(BF16)
     load_e.wait()
 
     def to_core(c):

time: 32.1 us -> 31.4 us (0.978)
  Pallas kernels: 30.5 us -> 29.8 us
    pallas_call x1, Pallas kernels: 30.5 us -> 29.8 us  [fused(): pl.pallas_call(functools.partial(kernel, n, chunks), out_shape=jax.ShapeD...]
where the time goes in v3:
time: 31.4 us; the launch traced here: 31.2 us
  Pallas kernels  29.8 us (95%)
  local copies, waits for them, and re-layouts  1.4 us (4%)
    pallas_call x1, Pallas kernels, fused(): pl.pallas_call(functools.partial(kernel, n, chunks), out_shape=jax.ShapeD...  29.8 us
    unnamed x1, local copies, waits for them, and re-layouts  1.4 us

profile of v3, /device:TPU:0, one launch (start us, length us, event | category | flops | bytes accessed | tf_op | source)
XLA Modules:
  0.0 31.2 jit_solution(14200392205219024808)
XLA Ops:
  0.0 29.8 %fused.1 = bf16[2,8192]{1,0:T(2,128)(2,1)} custom-call(s32[1,32]{1,0:T(1,128)} %bitcast.2, s32[1,16]{1,0:T(1,128)} %bitcast.3, bf16[32,1792]{1,0:T(8,128)(2,1)} %hid.1, bf16[1792,8192]{1,0:T(8,128)(2,1)} %w_hbm.1, bf16[1,64,28672]{2,1,0:T(8,128)(2,1)} %s_hbm.1, bf16[1,64,8192]{2,1,0:T(8,128)(2,1)} %e_hbm.1), custom_call_target="tpu_custom_call" | custom-call | tf_op jit(solution)/shard_map/fused/pallas_call | solution.py:219
  29.8 1.4 %copy.8 = bf16[2,8192]{1,0:T(2,128)(2,1)} copy(bf16[2,8192]{1,0:T(2,128)(2,1)} %fused.1) | data formatting | bytes 65536

commit v4 on v3

--- a/solution.py
+++ b/solution.py
@@ -27,7 +27,7 @@
 
 def kernel(n, chunks, vid, own, hid, w_hbm, s_hbm, e_hbm, out, wbuf, sbuf, ebuf, hperm, snd, rcv,
            part, arcv, bsnd, brcv, keep, csnd, crcv, wsem, ssem, esem, dss, drs, asem, arem, bsem,
-           brem, csem, crem):
+           brem, csem, crem, spread_out):
     me = lax.axis_index("tp")
     core, x, z = lax.rem(me, 2), lax.rem(me // 2, 2), me // 4
     nz = n // 4
@@ -122,8 +122,13 @@
             totals = shrink(d, totals)
     top, low = totals
     shrunk = (top[:CAP] + low[CAP:]).astype(BF16)
-    shrunk = contract(spread, shrunk, 1, 0).astype(BF16)
+    spread_out[...] = contract(spread, shrunk, 1, 0).astype(BF16).reshape(2, 2 * group, -1)
     load_e.wait()
+
+    def add_delta(c, to):
+        at = pl.ds(pl.multiple_of(c * wide, wide), wide)
+        delta = jnp.dot(spread_out[to], ebuf[:, at], preferred_element_type=F32)
+        part[c, to] = part[c, to] + delta.astype(BF16).astype(F32).reshape(2, group, wide)
 
     def to_core(c):
         return pltpu.make_async_remote_copy(
@@ -143,13 +148,12 @@
 
     @pl.loop(0, chunks)
     def _(c):
-        at = pl.ds(pl.multiple_of(c * wide, wide), wide)
-        delta = jnp.dot(shrunk, ebuf[:, at], preferred_element_type=F32).astype(BF16).astype(F32)
-        part[c] = part[c] + delta.reshape(2, 2, group, wide)
+        add_delta(c, 1 - core)
         to_core(c).start()
 
     @pl.loop(0, chunks)
     def _(c):
+        add_delta(c, core)
         to_core(c).wait_recv()
         away = part[c, core, 1 - x] + arcv[c, 1 - x]
         away = jnp.concatenate([away[:, :wide // 2], away[:, wide // 2:]], axis=0)
@@ -238,6 +242,7 @@
             dma((chunks,)), dma(()), dma(()), dma((n,)), dma((n,)),
             dma((chunks,)), dma((chunks,)), dma((chunks,)), dma((chunks,)),
             dma((chunks, nz - 1)), dma((chunks, nz - 1)),
+            pltpu.VMEM((2, 2 * group, rank), BF16),
         ],
         compiler_params=pltpu.CompilerParams(
             collective_id=0, has_side_effects=True, vmem_limit_bytes=56 * 2**20),

time: 31.4 us -> 31.4 us (level)
  no operation moved by 1% of the time
where the time goes in v4:
time: 31.4 us; the launch traced here: 31.2 us
  Pallas kernels  29.8 us (95%)
  local copies, waits for them, and re-layouts  1.4 us (4%)
    pallas_call x1, Pallas kernels, fused(): pl.pallas_call(functools.partial(kernel, n, chunks), out_shape=jax.ShapeD...  29.8 us
    unnamed x1, local copies, waits for them, and re-layouts  1.4 us

profile of v4, /device:TPU:0, one launch (start us, length us, event | category | flops | bytes accessed | tf_op | source)
XLA Modules:
  0.0 31.2 jit_solution(5312499526742059850)
XLA Ops:
  0.0 29.8 %fused.1 = bf16[2,8192]{1,0:T(2,128)(2,1)} custom-call(s32[1,32]{1,0:T(1,128)} %bitcast.2, s32[1,16]{1,0:T(1,128)} %bitcast.3, bf16[32,1792]{1,0:T(8,128)(2,1)} %hid.1, bf16[1792,8192]{1,0:T(8,128)(2,1)} %w_hbm.1, bf16[1,64,28672]{2,1,0:T(8,128)(2,1)} %s_hbm.1, bf16[1,64,8192]{2,1,0:T(8,128)(2,1)} %e_hbm.1), custom_call_target="tpu_custom_call" | custom-call | tf_op jit(solution)/shard_map/fused/pallas_call | solution.py:223
  29.8 1.4 %copy.8 = bf16[2,8192]{1,0:T(2,128)(2,1)} copy(bf16[2,8192]{1,0:T(2,128)(2,1)} %fused.1) | data formatting | bytes 65536
